TPU v7x, 256 devices: a whole 4x4x8 slice. The times are simulated.
256 devices in a mesh: dp: 32 (over x, y, core), expert: 8 (over z).
Axes of the slice: x: 4, y: 4, z: 8, core: 2. Of those that a mesh axis runs over, the one named last changes fastest.
Arguments:
- tokens: float32 [32768, 1280], P(('dp', 'expert')), may hold values from -6 to 6
- router_weight: float32 [1280, 32], replicated, may hold values from -0.3125 to 0.3125
- expert_in: float32 [32, 1280, 2560], P('dp', None, 'expert'), may hold values from -0.15625 to 0.15625
- expert_out: float32 [32, 2560, 1280], P('dp', 'expert'), may hold values from -0.125 to 0.125
- projection: float32 [2, 1280, 512], P(None, 'expert'), may hold values from -0.15625 to 0.15625
- assignment: int32 [32768], P(('dp', 'expert')), may hold values from 0 to 31, as said below
- modality: int32 [32768], P(('dp', 'expert')), may hold values from 0 to 1, as said below
Outputs:
- losses: float32 [3], replicated
- grad_tokens: float32 [32768, 1280], P(('dp', 'expert'))
- grad_router: float32 [1280, 32], replicated
- grad_expert_in: float32 [32, 1280, 2560], P('dp', None, 'expert')
- grad_expert_out: float32 [32, 2560, 1280], P('dp', 'expert')
- grad_projection: float32 [2, 1280, 512], P(None, 'expert')
Inputs may be any that keep to these rules, and one draw needn't show every extreme that they name: `assignment`: within each aligned block of 128 tokens (the tokens of one device) no expert is named by more than 5 tokens. In every block some expert is named exactly 5 times, and one expert is named 5 times in every block. Each aligned block of 128 tokens is one image-text pair: its image tokens come first, and it holds at least 16 tokens of each modality.
All inputs are finite; a program needn't handle non-finite values.
Results may differ from a plain program's by a relative error of at most 0.00013.
Values sent between devices are 32-bit elements; how exact they have to be, the bound alone decides.
No kernel may reach another device: no remote copies, remote signals or barrier semaphores. Data moves between devices by JAX's collectives and lax.ppermute only.
A program may use at most 192 MiB of HBM per device.

v0:
```python
import jax
import jax.numpy as jnp
from jax import lax
from jax.sharding import PartitionSpec as P

PAIR_LEN = 128


highest = lax.Precision.HIGHEST
contrast_scale = 10.0
entropy_weight = 0.5
norm_epsilon = 1e-06


def gelu_exact(values):
    return jax.nn.gelu(values, approximate=False)


def body(tokens, router_weight, expert_in, expert_out, projection, assignment, modality):
    tok_count, model_width = tokens.shape
    experts = router_weight.shape[1]
    capacity = 5 * tok_count // (4 * experts)
    pairs_dev = tok_count // PAIR_LEN
    slice_width = projection.shape[1]
    total_tokens = tok_count * lax.axis_size(("dp", "expert"))
    logits = jnp.dot(tokens, router_weight, precision=highest)
    exponent = jnp.exp(logits)
    router_prob = exponent / jnp.sum(exponent, axis=1, keepdims=True)
    expert_ids = lax.broadcasted_iota(jnp.int32, (1, experts), 1)
    chosen_int = (assignment[:, None] == expert_ids).astype(jnp.int32)
    chosen_mask = chosen_int.astype(jnp.float32)
    gate_value = jnp.sum(router_prob * chosen_mask, axis=1)
    earlier = jnp.cumsum(chosen_int, axis=0) - chosen_int
    slot = jnp.sum(earlier * chosen_int, axis=1)
    cell_ids = lax.broadcasted_iota(jnp.int32, (1, capacity * experts), 1)
    onehot = ((slot * experts + assignment)[:, None] == cell_ids).astype(jnp.float32)
    is_image = (modality == 0).astype(jnp.float32)
    modal_mask = jnp.stack([is_image, 1.0 - is_image], axis=1)
    usage_part = jnp.einsum("tm,te->me", modal_mask, router_prob, precision=highest)
    count_part = jnp.sum(modal_mask, axis=0)
    usage_sum, count_sum = lax.psum((usage_part, count_part), ("dp", "expert"))
    dispatched = jnp.einsum("tc,td->cd", onehot, tokens, precision=highest).reshape(
        capacity, experts, model_width
    )
    received = lax.all_to_all(dispatched, "dp", split_axis=1, concat_axis=0, tiled=True)
    routed_rows = lax.all_gather(received, "expert", axis=0, tiled=True)
    hidden_pre = jnp.einsum("red,edf->ref", routed_rows, expert_in, precision=highest)
    hidden = gelu_exact(hidden_pre)
    rows_part = hidden
    expert_result = lax.psum_scatter(
        jnp.einsum("ref,efd->red", rows_part, expert_out, precision=highest),
        "expert",
        scatter_dimension=0,
        tiled=True,
    )
    returned = lax.all_to_all(expert_result, "dp", split_axis=0, concat_axis=1, tiled=True)
    combined = jnp.dot(onehot, returned.reshape(capacity * experts, model_width), precision=highest)
    output = tokens + gate_value[:, None] * combined
    pair_owner = lax.broadcasted_iota(jnp.int32, (tok_count, 1), 0) // PAIR_LEN
    pair_ids = lax.broadcasted_iota(jnp.int32, (1, pairs_dev), 1)
    membership = (pair_owner == pair_ids).astype(jnp.float32)
    group_mask = (membership[:, :, None] * modal_mask[:, None, :]).reshape(tok_count, pairs_dev * 2)
    group_sizes = jnp.sum(group_mask, axis=0)
    pooled = (
        jnp.einsum("tg,td->gd", group_mask, output, precision=highest) / group_sizes[:, None]
    ).reshape(pairs_dev, 2, model_width)
    offset = lax.axis_index("expert") * slice_width
    pooled_all = lax.all_gather(pooled, "expert", axis=0, tiled=True)
    pooled_cut = lax.dynamic_slice_in_dim(pooled_all, offset, slice_width, 2)
    rows_part = pooled_cut
    embedding = lax.psum_scatter(
        jnp.einsum("pmd,mde->pme", rows_part, projection, precision=highest),
        "expert",
        scatter_dimension=0,
        tiled=True,
    )
    radius = jnp.sqrt(jnp.sum(embedding * embedding, axis=2, keepdims=True) + norm_epsilon)
    unit_embed = embedding / radius
    everyone = lax.all_gather(unit_embed, ("dp", "expert"), axis=0, tiled=True)
    total_pairs = everyone.shape[0]
    all_img = everyone[:, 0]
    all_txt = everyone[:, 1]
    own_img = unit_embed[:, 0]
    own_txt = unit_embed[:, 1]
    score_img = contrast_scale * jnp.einsum("pe,qe->pq", own_img, all_txt, precision=highest)
    score_txt = contrast_scale * jnp.einsum("pe,qe->pq", own_txt, all_img, precision=highest)
    log_total_img = jnp.log(jnp.sum(jnp.exp(score_img), axis=1))
    log_total_txt = jnp.log(jnp.sum(jnp.exp(score_txt), axis=1))
    matched = contrast_scale * jnp.sum(own_img * own_txt, axis=1)
    loss_part = jnp.sum(log_total_img + log_total_txt - 2.0 * matched)
    loss_sum = lax.psum(loss_part, ("dp", "expert"))
    weight_img = jnp.exp(score_img - log_total_img[:, None])
    weight_txt = jnp.exp(score_txt - log_total_txt[:, None])
    spread = jnp.stack(
        [
            jnp.einsum("pq,pe->qe", weight_txt, own_txt, precision=highest),
            jnp.einsum("pq,pe->qe", weight_img, own_img, precision=highest),
        ],
        axis=1,
    )
    cross_terms = lax.psum_scatter(spread, ("dp", "expert"), scatter_dimension=0, tiled=True)
    cross_img = cross_terms[:, 0]
    cross_txt = cross_terms[:, 1]
    coefficient = contrast_scale * total_tokens / (2.0 * total_pairs)
    grad_img = coefficient * (
        jnp.dot(weight_img, all_txt, precision=highest) + cross_img - 2.0 * own_txt
    )
    grad_txt = coefficient * (
        jnp.dot(weight_txt, all_img, precision=highest) + cross_txt - 2.0 * own_img
    )
    grad_unit = jnp.stack([grad_img, grad_txt], axis=1)
    grad_embed = (
        grad_unit - unit_embed * jnp.sum(unit_embed * grad_unit, axis=2, keepdims=True)
    ) / radius
    embed_grads_all = lax.all_gather(grad_embed, "expert", axis=0, tiled=True)
    projection_part = jnp.einsum("pmd,pme->mde", pooled_cut, embed_grads_all, precision=highest)
    grad_projection = lax.psum(projection_part, "dp")
    pooled_part = jnp.einsum("pme,mde->pmd", embed_grads_all, projection, precision=highest)
    grad_pooled = lax.all_to_all(pooled_part, "expert", split_axis=0, concat_axis=2, tiled=True)
    scaled_pooled = grad_pooled.reshape(pairs_dev * 2, model_width) / group_sizes[:, None]
    grad_output = jnp.dot(group_mask, scaled_pooled, precision=highest)
    grad_gate = jnp.sum(grad_output * combined, axis=1)
    grad_combined = gate_value[:, None] * grad_output
    grad_sent = jnp.einsum("tc,td->cd", onehot, grad_combined, precision=highest).reshape(
        capacity, experts, model_width
    )
    grad_received = lax.all_to_all(grad_sent, "dp", split_axis=1, concat_axis=0, tiled=True)
    unused_value, gelu_back = jax.vjp(gelu_exact, hidden_pre)
    grad_routed = lax.all_gather(grad_received, "expert", axis=0, tiled=True)
    grad_expert_out = jnp.einsum("ref,red->efd", hidden, grad_routed, precision=highest)
    grad_hidden = jnp.einsum("red,efd->ref", grad_routed, expert_out, precision=highest)
    grad_pre = gelu_back(grad_hidden)[0]
    grad_expert_in = jnp.einsum("red,ref->edf", routed_rows, grad_pre, precision=highest)
    rows_part = grad_pre
    grad_rows_in = lax.psum_scatter(
        jnp.einsum("ref,edf->red", rows_part, expert_in, precision=highest),
        "expert",
        scatter_dimension=0,
        tiled=True,
    )
    grad_back = lax.all_to_all(grad_rows_in, "dp", split_axis=0, concat_axis=1, tiled=True)
    grad_dispatch = jnp.dot(
        onehot, grad_back.reshape(capacity * experts, model_width), precision=highest
    )
    mean_usage = usage_sum / count_sum[:, None]
    log_usage = jnp.log(mean_usage)
    entropy_terms = jnp.sum(mean_usage * log_usage, axis=1)
    usage_factor = entropy_weight * total_tokens * (log_usage + 1.0) / count_sum[:, None]
    grad_prob = chosen_mask * grad_gate[:, None] + jnp.dot(
        modal_mask, usage_factor, precision=highest
    )
    grad_logits = router_prob * (
        grad_prob - jnp.sum(router_prob * grad_prob, axis=1, keepdims=True)
    )
    router_part = jnp.einsum("td,te->de", tokens, grad_logits, precision=highest)
    grad_router = lax.psum(router_part, ("dp", "expert"))
    grad_tokens = (
        grad_output
        + grad_dispatch
        + jnp.einsum("te,de->td", grad_logits, router_weight, precision=highest)
    )
    losses = jnp.stack([loss_sum / (2.0 * total_pairs), entropy_terms[0], entropy_terms[1]])
    return (losses, grad_tokens, grad_router, grad_expert_in, grad_expert_out, grad_projection)


def solution(mesh):
    return jax.shard_map(
        body,
        mesh=mesh,
        in_specs=(
            P(("dp", "expert"), None),
            P(),
            P("dp", None, "expert"),
            P("dp", "expert", None),
            P(None, "expert", None),
            P(("dp", "expert")),
            P(("dp", "expert")),
        ),
        out_specs=(
            P(),
            P(("dp", "expert"), None),
            P(),
            P("dp", None, "expert"),
            P("dp", "expert", None),
            P(None, "expert", None),
        ),
        check_vma=False,
    )
```

profile of v0, /device:TPU:1, one launch (start us, length us, event | category | flops | bytes accessed | tf_op | source)
XLA Modules:
  0.0 1290.0 jit_solution(4363798688961456634)
XLA Ops:
  11.9 28.6 %all_to_all.78 = f32[5,32,1280]{2,0,1:T(8,128)S(1)} all-to-all(f32[5,32,1280]{2,0,1:T(8,128)S(1)} %copy.52), channel_id=1, replica_groups=mesh['dp'=32,'expert'=8] {'dp'}, dimensions={1} | all-to-all | bytes 1638400 | tf_op jit(solution)/shard_map/all_to_all | solution.py:45
  42.6 75.9 %all-gather.6.cloned.1.call-done = f32[1280,1,1280]{2,1,0:T(1,128)} async-done(((f32[160,1,1280]{2,1,0:T(1,128)}), f32[1280,1,1280]{2,1,0:T(1,128)}) %all-gather.6.cloned.1.call-update) | async-done | bytes 6553616 | tf_op jit(solution)/shard_map/all_gather | solution.py:46
  118.5 9.8 fusion.6
  129.5 15.8 %convolution_bitcast_fusion.1 = f32[1280,1,1280]{2,0,1:T(8,128)} fusion(f32[1,320,1280]{2,1,0:T(8,128)S(1)} %copy-done, f32[1280,320]{0,1:T(8,128)S(1)} %fusion.6), kind=kOutput, calls=%fused_computation.1 | convolution fusion | flops 6317670400 | bytes 9830400 | tf_op jit(solution)/shard_map/ref,efd->red/dot_general | solution.py:51
  146.6 75.1 %reduce-scatter.3.cloned.1.call-done = f32[160,1,1280]{2,0,1:T(8,128)} async-done(((f32[1280,1,1280]{2,0,1:T(8,128)}), f32[160,1,1280]{2,0,1:T(8,128)}) %reduce-scatter.3.cloned.1.call-update) | async-done | bytes 819216 | tf_op jit(solution)/shard_map/reduce_scatter | solution.py:50
  224.6 7.6 all-to-all-start.1
  233.2 13.5 %all-to-all-done.1 = f32[160,1,1280]{2,1,0:T(1,128)S(1)} async-done(((f32[160,1,1280]{2,1,0:T(1,128)}), f32[160,1,1280]{2,1,0:T(1,128)S(1)}, u32[]{:S(2)}, u32[]{:S(2)}) %all-to-all-start.1) | async-done | bytes 819232 | tf_op jit(solution)/shard_map/all_to_all | solution.py:56
  247.8 18.2 %all-gather.1 = f32[8,2,1280]{2,1,0:T(2,128)S(1)} all-gather(f32[1,2,1280]{2,1,0:T(2,128)S(1)} %fusion.21), channel_id=2, replica_groups=mesh['dp'=32,'expert'=8] {'expert'}, dimensions={0}, use_global_device_ids=true | all-gather | bytes 92160 | tf_op jit(solution)/shard_map/all_gather | solution.py:68
  266.6 21.4 %all-reduce = f32[8,2,512]{2,1,0:T(2,128)S(1)} all-reduce(f32[8,2,512]{2,1,0:T(2,128)S(1)} %copy.58), channel_id=4, replica_groups=mesh['dp'=32,'expert'=8] {'expert'}, use_global_device_ids=true, to_apply=%region_6.7.clone | all-reduce | flops 8192 | bytes 65536
  291.8 110.4 %all-gather.8.cloned.1.call-done = f32[256,2,512]{2,1,0:T(2,128)} async-done(((f32[1,2,512]{2,1,0:T(2,128)}), f32[256,2,512]{2,1,0:T(2,128)}) %all-gather.8.cloned.1.call-update) | async-done | bytes 1048592 | tf_op jit(solution)/shard_map/all_gather | solution.py:79
  412.0 252.7 %all-reduce.11.cloned.1.call-done = f32[256,2,512]{2,1,0:T(2,128)} async-done(((f32[256,2,512]{2,1,0:T(2,128)}), f32[256,2,512]{2,1,0:T(2,128)}) %all-reduce.11.cloned.1.call-update) | async-done | bytes 1048592
  667.0 18.8 %all_gather.18 = f32[8,2,512]{2,1,0:T(2,128)S(1)} all-gather(f32[1,2,512]{2,1,0:T(2,128)S(1)} %subtract_divide_fusion), channel_id=1, replica_groups=mesh['dp'=32,'expert'=8] {'expert'}, dimensions={0}, use_global_device_ids=true | all-gather | bytes 36864 | tf_op jit(solution)/shard_map/all_gather | solution.py:115
  687.6 12.4 all_to_all.79
  703.0 34.3 %all_to_all.80 = f32[5,32,1280]{2,0,1:T(8,128)S(1)} all-to-all(f32[5,32,1280]{2,0,1:T(8,128)S(1)} %copy.62), channel_id=1, replica_groups=mesh['dp'=32,'expert'=8] {'dp'}, dimensions={1} | all-to-all | bytes 1638400 | tf_op jit(solution)/shard_map/all_to_all | solution.py:127
  739.7 69.0 %all-gather.10.cloned.1.call-done = f32[1280,1,1280]{2,1,0:T(1,128)} async-done(((f32[160,1,1280]{2,1,0:T(1,128)}), f32[1280,1,1280]{2,1,0:T(1,128)}) %all-gather.10.cloned.1.call-update) | async-done | bytes 6553616 | tf_op jit(solution)/shard_map/all_gather | solution.py:129
  808.7 12.8 fusion.30
  821.5 14.1 %convolution_bitcast_fusion = f32[1280,1,1280]{2,0,1:T(8,128)} fusion(f32[1280,1,320]{0,2,1:T(8,128)S(1)} %fusion.30, f32[1,1280,320]{1,2,0:T(8,128)} %param.9), kind=kOutput, calls=%fused_computation | convolution fusion | flops 6291456000 | bytes 9830400 | tf_op jit(solution)/shard_map/ref,edf->red/dot_general | solution.py:136
  836.5 80.0 %all-reduce.2 = (f32[2,32]{1,0:T(2,128)S(1)}, f32[2]{0:T(128)S(1)}, f32[]{:T(128)}) all-reduce(f32[2,32]{1,0:T(2,128)S(1)} %fusion.168, f32[2]{0:T(128)S(1)} %get-tuple-element.7, f32[]{:T(128)S(6)} %sub.62), channel_id=1, replica_groups=mesh['dp'=32,'expert'=8] {'dp','expert'}, use_global_device_ids=true, to_apply=%region_12.13 | all-reduce | flops 67 | bytes 536 | tf_op jit(solution)/shard_map/psum | solution.py:41
  922.2 2.9 copy.65
  925.1 5.3 all-to-all-start.4
  930.4 14.9 %fusion.18 = f32[1,320,1280]{2,1,0:T(8,128)} fusion(f32[1280,1,1280]{2,1,0:T(1,128)} %all-gather.10.cloned.1.call-done, f32[1280,320]{0,1:T(8,128)} %copy-done.6), kind=kOutput, calls=%fused_computation.16 | convolution fusion | flops 6317670400 | bytes 9830400 | tf_op jit(solution)/shard_map/ref,red->efd/dot_general | solution.py:130
  945.3 11.3 fusion.12
  960.1 204.7 %all-reduce.7.cloned.1.call-done = f32[1280,32]{0,1:T(8,128)} async-done(((f32[1280,32]{0,1:T(8,128)}), f32[1280,32]{0,1:T(8,128)}) %all-reduce.7.cloned.1.call-update) | async-done | bytes 163856 | tf_op jit(solution)/shard_map/psum | solution.py:156
  1164.8 114.4 %all-reduce.9.cloned.1.call-done = f32[2,160,512]{2,1,0:T(8,128)} async-done(((f32[2,160,512]{2,1,0:T(8,128)}), f32[2,160,512]{2,1,0:T(8,128)}) %all-reduce.9.cloned.1.call-update) | async-done | bytes 655376 | tf_op jit(solution)/shard_map/psum | solution.py:117
  (112 shorter events, 48.4 us)
Async XLA Ops:
  7.2 122.4 %copy-start = (f32[1,320,1280]{2,1,0:T(8,128)S(1)}, f32[1,320,1280]{2,1,0:T(8,128)}, u32[]{:S(2)}) copy-start(f32[1,320,1280]{2,1,0:T(8,128)} %param.10) | copy-start | bytes 4915204
  7.2 111.3 %all-gather.6.cloned.1.call-start = ((), (), s32[]{:S(2)}) async-start(), calls=%async_computation.7 | async-start | bytes 7372800 | tf_op jit(solution)/shard_map/all_gather | solution.py:46
  40.8 77.8 %copy-start.2 = (f32[1,1280,320]{1,2,0:T(8,128)S(1)}, f32[1,1280,320]{1,2,0:T(8,128)}, u32[]{:S(2)}) copy-start(f32[1,1280,320]{1,2,0:T(8,128)} %param.9) | copy-start | bytes 4915204
  42.5 179.2 %reduce-scatter.3.cloned.1.call-start = ((), (), s32[]{:S(2)}) async-start(), calls=%async_computation.8 | async-start | bytes 7372800 | tf_op jit(solution)/shard_map/reduce_scatter | solution.py:50
  128.4 1.2 copy-start.6
  145.3 0.7 copy-start.12
  145.3 1.3 copy-start.11
  146.6 85.9 %copy-start.1 = (f32[128,1280]{1,0:T(8,128)S(1)}, f32[128,1280]{1,0:T(8,128)}, u32[]{:S(2)}) copy-start(f32[128,1280]{1,0:T(8,128)} %param.7) | copy-start | bytes 1966084
  146.6 85.9 %copy-start.7 = (f32[1280,32]{0,1:T(8,128)S(1)}, f32[1280,32]{0,1:T(8,128)}, u32[]{:S(2)}) copy-start(f32[1280,32]{0,1:T(8,128)} %param.8) | copy-start | bytes 491524
  224.6 8.6 copy-start.10
  224.6 22.2 %all-to-all-start.1 = ((f32[160,1,1280]{2,1,0:T(1,128)}), f32[160,1,1280]{2,1,0:T(1,128)S(1)}, u32[]{:S(2)}, u32[]{:S(2)}) async-start(f32[160,1,1280]{2,1,0:T(1,128)} %copy.55), calls=%async_computation.2 | async-start | bytes 1638400 | tf_op jit(solution)/shard_map/all_to_all | solution.py:56
  232.2 170.0 %all-gather.8.cloned.1.call-start = ((), (), s32[]{:S(2)}) async-start(), calls=%async_computation.9 | async-start | bytes 1052672 | tf_op jit(solution)/shard_map/all_gather | solution.py:79
  246.8 19.4 %copy-start.5 = (f32[2,160,512]{2,1,0:T(8,128)S(1)}, f32[2,160,512]{2,1,0:T(8,128)}, u32[]{:S(2)}) copy-start(f32[2,160,512]{2,1,0:T(8,128)} %param.11) | copy-start | bytes 1966084
  290.1 114.5 %copy-start.9 = (f32[1,2,512]{2,1,0:T(2,128)S(1)}, f32[1,2,512]{2,1,0:T(2,128)}, u32[]{:S(2)}) copy-start(f32[1,2,512]{2,1,0:T(2,128)} %dynamic-slice_divide_fusion) | copy-start | bytes 12292
  290.2 374.5 %all-reduce.11.cloned.1.call-start = ((), (), s32[]{:S(2)}) async-start(), calls=%async_computation.14 | async-start | bytes 2097152
  411.3 397.4 %all-gather.10.cloned.1.call-start = ((), (), s32[]{:S(2)}) async-start(), calls=%async_computation.10 | async-start | bytes 7372800 | tf_op jit(solution)/shard_map/all_gather | solution.py:129
  701.0 0.8 copy-start.3
  739.3 182.9 %reduce-scatter.5.cloned.1.call-start = ((), (), s32[]{:S(2)}) async-start(), calls=%async_computation.11 | async-start | bytes 7372800 | tf_op jit(solution)/shard_map/reduce_scatter | solution.py:135
  835.7 329.1 %all-reduce.7.cloned.1.call-start = ((), (), s32[]{:S(2)}) async-start(), calls=%async_computation.12 | async-start | bytes 327680 | tf_op jit(solution)/shard_map/psum | solution.py:156
  920.5 358.6 %all-reduce.9.cloned.1.call-start = ((), (), s32[]{:S(2)}) async-start(), calls=%async_computation.13 | async-start | bytes 1310720 | tf_op jit(solution)/shard_map/psum | solution.py:117
  925.1 31.5 %all-to-all-start.4 = ((f32[160,1,1280]{2,1,0:T(1,128)}), f32[160,1,1280]{2,1,0:T(1,128)}, u32[]{:S(2)}, u32[]{:S(2)}) async-start(f32[160,1,1280]{2,1,0:T(1,128)} %copy.65), calls=%async_computation.6 | async-start | bytes 1638400 | tf_op jit(solution)/shard_map/all_to_all | solution.py:141
  956.6 1.3 copy-start.4
  956.6 1.9 copy-start.8
Sparse Core Ops, SparseCore 0:
  42.7 75.8 all-gather.5
  145.4 76.2 reduce-scatter.2
  290.3 111.8 all-gather.7
  411.4 253.2 all-reduce.10
  739.4 69.2 all-gather.9
  835.8 77.6 reduce-scatter.4
  920.7 244.0 all-reduce.6
  1168.4 110.7 all-reduce.8
where the time goes:
time: 1300 us; the launch traced here: 1290 us
  waiting for transfers between devices  916 us (70%)
  blocking collectives  214 us (16%)
  matrix products  93.9 us (7%)
  local copies, waits for them, and re-layouts  23.4 us (2%)
  between operations  17.6 us (1%)
  starting transfers between devices  13.8 us (1%)
    unnamed x9, waiting for transfers between devices  253 us
    psum x1, waiting for transfers between devices, body(): grad_router = lax.psum(router_part, ('dp', 'expert'))  205 us
    psum x1, waiting for transfers between devices, body(): grad_projection = lax.psum(projection_part, 'dp')  114 us
    all_gather x1, waiting for transfers between devices, body(): everyone = lax.all_gather(unit_embed, ('dp', 'expert'), axis=0, tiled=True)  110 us
    psum x1, blocking collectives, body(): usage_sum, count_sum = lax.psum((usage_part, count_part), ('dp', 'expert'))  80 us
    all_gather x1, waiting for transfers between devices, body(): routed_rows = lax.all_gather(received, 'expert', axis=0, tiled=True)  75.9 us
    reduce_scatter x1, waiting for transfers between devices, body(): lax.psum_scatter(jnp.einsum('ref,efd->red', rows_part, expert_out, precis...  75.1 us
    all_gather x1, waiting for transfers between devices, body(): grad_routed = lax.all_gather(grad_received, 'expert', axis=0, tiled=True)  69 us
  transfers between devices with their start and end apart: 10, of which 8 were waited for; matrix products, arithmetic and copies ran while one was open for 3% of the time, Pallas kernels for 0%

commit v1 on v0

v1 whole, which is shorter than its diff:
```python
import jax
import jax.numpy as jnp
from jax import lax
from jax.sharding import PartitionSpec as P

highest = lax.Precision.HIGHEST
high = lax.Precision.HIGH
contrast_scale = 10.0
entropy_weight = 0.5
norm_epsilon = 1e-06
CAP = 5


def gelu_exact(values):
    return jax.nn.gelu(values, approximate=False)


def dot(a, b, dims, precision=high):
    return lax.dot_general(a, b, (dims, ((), ())), precision=precision)


def mm(a, b, precision=high):
    return dot(a, b, ((1,), (0,)), precision)


def mm_nt(a, b, precision=high):
    return dot(a, b, ((1,), (1,)), precision)


def mm_tn(a, b, precision=high):
    return dot(a, b, ((0,), (0,)), precision)


def a2a(values, axis_name, axis):
    return lax.all_to_all(values, axis_name, split_axis=axis, concat_axis=axis, tiled=True)


def gather(values, axis_name):
    return lax.all_gather(values, axis_name, axis=0, tiled=True)


def body(tokens, router_weight, expert_in, expert_out, projection, assignment, modality):
    tok_count, width = tokens.shape
    experts = router_weight.shape[1]
    n_dp = lax.axis_size("dp")
    n_z = lax.axis_size("expert")
    pairs = n_dp * n_z
    total_tokens = tok_count * pairs
    w_in = expert_in[0]
    w_out = expert_out[0]
    hidden_dev = w_in.shape[1]
    embed_width = projection.shape[2]
    my_dp = lax.axis_index("dp")
    my_z = lax.axis_index("expert")
    own_pair = my_z * n_dp + my_dp
    my_core = my_dp % 2

    projection_mine = gather(jnp.where(my_core == 0, projection[0], projection[1]), "expert")
    projection_other = lax.ppermute(projection_mine, "dp", [(i, i ^ 1) for i in range(n_dp)])

    expert_ids = lax.broadcasted_iota(jnp.int32, (1, experts), 1)
    chosen_mask = (assignment[:, None] == expert_ids).astype(jnp.float32)
    before = (
        lax.broadcasted_iota(jnp.int32, (tok_count, tok_count), 0)
        > lax.broadcasted_iota(jnp.int32, (tok_count, tok_count), 1)
    ).astype(jnp.bfloat16)
    earlier = jnp.dot(
        before, chosen_mask.astype(jnp.bfloat16), preferred_element_type=jnp.float32
    )
    slot = jnp.sum(earlier * chosen_mask, axis=1).astype(jnp.int32)
    cell_ids = lax.broadcasted_iota(jnp.int32, (1, CAP * experts), 1)
    onehot = ((slot * experts + assignment)[:, None] == cell_ids).astype(jnp.float32)
    dispatched = mm_tn(onehot, tokens, highest).reshape(CAP, experts, width)
    received = a2a(dispatched, "dp", 1).reshape(CAP * n_dp, width)
    rows = gather(received, "expert")

    logits = mm(tokens, router_weight, highest)
    exponent = jnp.exp(logits)
    router_prob = exponent / jnp.sum(exponent, axis=1, keepdims=True)
    is_image = (modality == 0).astype(jnp.float32)
    modal_mask = jnp.stack([is_image, 1.0 - is_image], axis=0)
    images = jnp.sum(is_image)
    group_sizes = jnp.stack([images, tok_count - images])
    usage_part = mm(modal_mask, router_prob, highest).reshape(1, 2 * experts)
    image_slots = dot(chosen_mask, is_image, ((0,), (0,)), highest)
    meta = jnp.concatenate(
        [
            image_slots[:, None],
            jnp.broadcast_to(images, (experts, 1)),
            jnp.broadcast_to(usage_part, (experts, 2 * experts)),
            jnp.zeros((experts, 126 - 2 * experts), jnp.float32),
        ],
        axis=1,
    )
    meta, received_late = lax.optimization_barrier((meta, received[:1, :1]))
    meta_all = gather(a2a(meta, "dp", 0), "expert")
    token_means = mm(modal_mask / group_sizes[:, None], tokens, highest)

    projection_img = jnp.where(my_core == 0, projection_mine, projection_other)
    projection_txt = jnp.where(my_core == 0, projection_other, projection_mine)
    mixed_img = mm(w_out, projection_img)
    mixed_txt = mm(w_out, projection_txt)
    embed_means = jnp.concatenate(
        [mm(token_means[:1], projection_img), mm(token_means[1:], projection_txt)], axis=0
    )

    usage_all = jnp.sum(meta_all[:, 2 : 2 + 2 * experts], axis=0).reshape(2, experts)
    images_of = meta_all[:, 1]
    image_total = jnp.sum(images_of)
    count_sum = jnp.stack([image_total, total_tokens - image_total])
    slot_ids = lax.broadcasted_iota(jnp.int32, (1, CAP, 1), 1).astype(jnp.float32)
    in_image = slot_ids < meta_all[:, 0].reshape(n_z, 1, n_dp)
    weight_img = jnp.where(in_image, 1.0 / images_of.reshape(n_z, 1, n_dp), 0.0)
    weight_txt = jnp.where(in_image, 0.0, 1.0 / (tok_count - images_of).reshape(n_z, 1, n_dp))

    pre = mm(rows, w_in)
    row_exponent = jnp.exp(mm(rows, router_weight))
    row_prob = row_exponent / jnp.sum(row_exponent, axis=1, keepdims=True)
    my_expert = (expert_ids == my_dp).astype(jnp.float32)
    row_gate = jnp.sum(row_prob * my_expert, axis=1).reshape(n_z, CAP, n_dp)
    hidden, gelu_back = jax.vjp(gelu_exact, pre)
    hidden_rows = hidden.reshape(n_z, CAP, n_dp, hidden_dev)
    gate_img = (row_gate * weight_img)[..., None]
    gate_txt = (row_gate * weight_txt)[..., None]
    sum_img = jnp.sum(hidden_rows * gate_img, axis=1).reshape(pairs, hidden_dev)
    sum_txt = jnp.sum(hidden_rows * gate_txt, axis=1).reshape(pairs, hidden_dev)

    part = jnp.stack(
        [
            mm(sum_img, mixed_img).reshape(n_z, n_dp, embed_width),
            mm(sum_txt, mixed_txt).reshape(n_z, n_dp, embed_width),
        ],
        axis=1,
    )
    part = jnp.sum(a2a(part, "expert", 0), axis=0)
    embedding = jnp.sum(a2a(part, "dp", 1), axis=1) + embed_means
    column = lax.all_gather(embedding, "dp", axis=1, tiled=False)
    every = gather(column[None], "expert")
    embed_img = every[:, 0].reshape(pairs, embed_width)
    embed_txt = every[:, 1].reshape(pairs, embed_width)

    def normalized(values):
        radius = jnp.sqrt(jnp.sum(values * values, axis=1, keepdims=True) + norm_epsilon)
        return values / radius, radius

    unit_img, radius_img = normalized(embed_img)
    unit_txt, radius_txt = normalized(embed_txt)
    scores = contrast_scale * mm_nt(unit_img, unit_txt, highest)
    exp_scores = jnp.exp(scores)
    total_img = jnp.sum(exp_scores, axis=1, keepdims=True)
    total_txt = jnp.sum(exp_scores, axis=0, keepdims=True)
    diagonal = (
        lax.broadcasted_iota(jnp.int32, (pairs, pairs), 0)
        == lax.broadcasted_iota(jnp.int32, (pairs, pairs), 1)
    ).astype(jnp.float32)
    contrast = (
        jnp.sum(jnp.log(total_img)) + jnp.sum(jnp.log(total_txt)) - 2.0 * jnp.sum(scores * diagonal)
    ) / (2.0 * pairs)
    coupling = (exp_scores / total_img + exp_scores / total_txt - 2.0 * diagonal) * (
        contrast_scale * total_tokens / (2.0 * pairs)
    )

    def embed_back(unit, radius, grad_unit):
        return (grad_unit - unit * jnp.sum(unit * grad_unit, axis=1, keepdims=True)) / radius

    grad_img = embed_back(unit_img, radius_img, mm(coupling, unit_txt, highest))
    grad_txt = embed_back(unit_txt, radius_txt, mm_tn(coupling, unit_img, highest))

    back_img = mm_nt(grad_img, mixed_img).reshape(n_z, 1, n_dp, hidden_dev)
    back_txt = mm_nt(grad_txt, mixed_txt).reshape(n_z, 1, n_dp, hidden_dev)
    grad_hidden = gate_img * back_img + gate_txt * back_txt
    grad_pre = gelu_back(grad_hidden.reshape(pre.shape))[0]
    grad_log_gate = jnp.sum(hidden_rows * grad_hidden, axis=3).reshape(-1, 1)
    grad_row_logits = grad_log_gate * (my_expert - row_prob)
    grad_rows = mm_nt(grad_pre, w_in) + mm_nt(grad_row_logits, router_weight)
    grad_rows = lax.psum_scatter(grad_rows, "expert", scatter_dimension=0, tiled=True)
    grad_back = a2a(grad_rows.reshape(CAP, n_dp, width), "dp", 1).reshape(CAP * experts, width)
    grad_dispatch = mm(onehot, grad_back, highest)

    mean_usage = usage_all / count_sum[:, None]
    log_usage = jnp.log(mean_usage)
    entropy_terms = jnp.sum(mean_usage * log_usage, axis=1)
    usage_factor = entropy_weight * total_tokens * (log_usage + 1.0) / count_sum[:, None]
    grad_prob = mm_tn(modal_mask, usage_factor, highest)
    grad_logits = router_prob * (
        grad_prob - jnp.sum(router_prob * grad_prob, axis=1, keepdims=True)
    )

    grad_expert_in = mm_tn(rows, grad_pre)
    grad_expert_out = mm_nt(mm_tn(sum_img, grad_img), projection_img) + mm_nt(
        mm_tn(sum_txt, grad_txt), projection_txt
    )
    router_part = mm_tn(grad_row_logits, rows) + mm_tn(grad_logits, tokens)
    router_cut = jnp.sum(a2a(router_part, "dp", 0), axis=0, keepdims=True)
    router_cut = jnp.sum(gather(router_cut, "expert"), axis=0, keepdims=True)
    grad_router = gather(router_cut, "dp").T

    own = (lax.broadcasted_iota(jnp.int32, (1, pairs), 1) == own_pair).astype(jnp.float32)
    pooled_part = jnp.concatenate(
        [
            dot(w_out, sum_img, ((0,), (1,))) + token_means[0][:, None] * own,
            dot(w_out, sum_txt, ((0,), (1,))) + token_means[1][:, None] * own,
        ],
        axis=1,
    )
    pooled_cut = lax.psum_scatter(pooled_part, "expert", scatter_dimension=0, tiled=True)
    projection_part = jnp.concatenate(
        [mm(pooled_cut[:, :pairs], grad_img), mm(pooled_cut[:, pairs:], grad_txt)], axis=0
    )
    cut_rows = projection_part.shape[0] // n_dp
    projection_cut = jnp.sum(
        a2a(projection_part.reshape(n_dp, cut_rows, embed_width), "dp", 0), axis=0, keepdims=True
    )
    grad_projection = gather(projection_cut, "dp").reshape(projection.shape)

    own_img = lax.dynamic_slice_in_dim(grad_img, own_pair, 1, 0)
    own_txt = lax.dynamic_slice_in_dim(grad_txt, own_pair, 1, 0)
    grad_pooled = jnp.concatenate(
        [mm_nt(own_img, projection_img), mm_nt(own_txt, projection_txt)], axis=0
    )
    grad_output = mm_tn(modal_mask, grad_pooled / group_sizes[:, None], highest)
    grad_tokens = grad_output + mm_nt(grad_logits, router_weight, highest) + grad_dispatch
    losses = jnp.stack([contrast, entropy_terms[0], entropy_terms[1]])
    return (
        losses,
        grad_tokens,
        grad_router,
        grad_expert_in[None],
        grad_expert_out[None],
        grad_projection,
    )


def solution(mesh):
    return jax.shard_map(
        body,
        mesh=mesh,
        in_specs=(
            P(("dp", "expert"), None),
            P(),
            P("dp", None, "expert"),
            P("dp", "expert", None),
            P(None, "expert", None),
            P(("dp", "expert")),
            P(("dp", "expert")),
        ),
        out_specs=(
            P(),
            P(("dp", "expert"), None),
            P(),
            P("dp", None, "expert"),
            P("dp", "expert", None),
            P(None, "expert", None),
        ),
        check_vma=False,
    )
```

time: 1300 us -> 512 us (0.39)
  waiting for transfers between devices: 916 us -> 131 us
  blocking collectives: 214 us -> 147 us
  starting transfers between devices: 13.8 us -> 52.2 us
  other arithmetic: 11.8 us -> 30.2 us
    psum x2 -> x0, waiting for transfers between devices: 319 us -> none  [the longest x1 205 us: body(): grad_router = lax.psum(router_part, ('dp', 'expert'))]
    unnamed x9 -> x6, waiting for transfers between devices: 253 us -> 0.08 us
    all_gather x3, waiting for transfers between devices: 255 us -> 60.1 us  [gather(): return lax.all_gather(values, axis_name, axis=0, tiled=True)]
    all_gather x2 -> x5, blocking collectives: 37 us -> 118 us  [the longest x4 95.2 us: gather(): return lax.all_gather(values, axis_name, axis=0, tiled=True)]
    psum x1 -> x0, blocking collectives: 80 us -> none  [body(): usage_sum, count_sum = lax.psum((usage_part, count_part), ('dp', 'expert'))]
    all_to_all x3 -> x1, blocking collectives: 75.3 us -> 28.6 us  [a2a(): lax.all_to_all(values, axis_name, split_axis=axis, concat_axis=axis, tile...]
    reduce_scatter x2 -> x1, waiting for transfers between devices: 75.2 us -> 39.6 us  [body(): lax.psum_scatter(grad_rows, 'expert', scatter_dimension=0, tiled=True)]
    all_to_all x2 -> x6, starting transfers between devices: 12.9 us -> 48.3 us  [a2a(): lax.all_to_all(values, axis_name, split_axis=axis, concat_axis=axis, tile...]
  transfers between devices with their start and end apart: 10 -> 12, of which waited for: 8 -> 7; matrix products, arithmetic and copies ran while one was open for 3% -> 22% of each run, Pallas kernels for 0% -> 0%
where the time goes in v1:
time: 512 us; the launch traced here: 503 us
  blocking collectives  147 us (29%)
  waiting for transfers between devices  131 us (26%)
  matrix products  90.3 us (18%)
  starting transfers between devices  52.2 us (10%)
  local copies, waits for them, and re-layouts  34.6 us (7%)
  other arithmetic  30.2 us (6%)
  between operations  18.2 us (4%)
    all_gather x4, blocking collectives, gather(): return lax.all_gather(values, axis_name, axis=0, tiled=True)  95.2 us
    dot_general x37, matrix products, dot(): return lax.dot_general(a, b, (dims, ((), ())), precision=precision)  89.4 us
    all_gather x3, waiting for transfers between devices, gather(): return lax.all_gather(values, axis_name, axis=0, tiled=True)  60.1 us
    all_to_all x6, starting transfers between devices, a2a(): lax.all_to_all(values, axis_name, split_axis=axis, concat_axis=axis, tile...  48.3 us
    reduce_scatter x1, waiting for transfers between devices, body(): lax.psum_scatter(grad_rows, 'expert', scatter_dimension=0, tiled=True)  39.6 us
    all_to_all x6, waiting for transfers between devices, a2a(): lax.all_to_all(values, axis_name, split_axis=axis, concat_axis=axis, tile...  31.5 us
    all_to_all x1, blocking collectives, a2a(): lax.all_to_all(values, axis_name, split_axis=axis, concat_axis=axis, tile...  28.6 us
    all_gather x1, blocking collectives, body(): column = lax.all_gather(embedding, 'dp', axis=1, tiled=False)  23 us
  transfers between devices with their start and end apart: 12, of which 7 were waited for; matrix products, arithmetic and copies ran while one was open for 22% of the time, Pallas kernels for 0%

profile of v1, /device:TPU:1, one launch (start us, length us, event | category | flops | bytes accessed | tf_op | source)
XLA Modules:
  0.0 503.4 jit_solution(17521257939773477270)
XLA Ops:
  12.0 28.6 %all_to_all.46 = f32[5,32,1280]{2,0,1:T(8,128)S(1)} all-to-all(f32[5,32,1280]{2,0,1:T(8,128)S(1)} %copy.42), channel_id=1, replica_groups=mesh['dp'=32,'expert'=8] {'dp'}, dimensions={1} | all-to-all | bytes 1638400 | tf_op jit(solution)/shard_map/all_to_all | solution.py:35
  41.8 11.8 %all-gather.15.cloned.1.call-done = f32[1,1280,512]{2,1,0:T(8,128)} async-done(((f32[1,160,512]{2,1,0:T(8,128)}), f32[1,1280,512]{2,1,0:T(8,128)}) %all-gather.15.cloned.1.call-update) | async-done | bytes 2621456 | tf_op jit(solution)/shard_map/all_gather | solution.py:39
  60.4 7.0 %all-to-all-start.1 = ((f32[32,1,128]{2,1,0:T(1,128)}), f32[32,1,128]{2,1,0:T(1,128)S(1)}, u32[]{:S(2)}, u32[]{:S(2)}) async-start(f32[32,1,128]{2,1,0:T(1,128)} %bitcast.9), calls=%async_computation.1 | async-start | bytes 32768 | tf_op jit(solution)/shard_map/all_to_all | solution.py:35
  68.0 6.3 %all-to-all-done.1 = f32[32,1,128]{2,1,0:T(1,128)S(1)} async-done(((f32[32,1,128]{2,1,0:T(1,128)}), f32[32,1,128]{2,1,0:T(1,128)S(1)}, u32[]{:S(2)}, u32[]{:S(2)}) %all-to-all-start.1) | async-done | bytes 16416 | tf_op jit(solution)/shard_map/all_to_all | solution.py:35
  74.3 21.2 %all-gather = f32[256,1,128]{2,1,0:T(1,128)S(1)} all-gather(f32[32,1,128]{2,1,0:T(1,128)S(1)} %all-to-all-done.1), channel_id=2, replica_groups=mesh['dp'=32,'expert'=8] {'expert'}, dimensions={0}, use_global_device_ids=true | all-gather | bytes 147456 | tf_op jit(solution)/shard_map/all_gather | solution.py:39
  105.5 30.2 %all-gather.13.cloned.1.call-done = f32[1280,1280]{1,0:T(8,128)} async-done(((f32[160,1280]{1,0:T(8,128)}), f32[1280,1280]{1,0:T(8,128)}) %all-gather.13.cloned.1.call-update) | async-done | bytes 6553616 | tf_op jit(solution)/shard_map/all_gather | solution.py:39
  135.7 5.8 %fusion.84 = (f32[1280]{0:T(1024)S(1)}, f32[1280,32]{0,1:T(8,128)S(1)}) fusion(f32[1280,1280]{1,0:T(8,128)} %all-gather.13.cloned.1.call-done, f32[1280,32]{0,1:T(8,128)} %param.8), kind=kOutput, calls=%fused_computation.174 | convolution fusion | flops 314612480 | bytes 6886400 | tf_op jit(solution)/shard_map/dot_general | solution.py:19
  142.3 13.6 %multiply_multiply_fusion.5 = (f32[1280,320]{0,1:T(8,128)}, f32[1280,320]{0,1:T(8,128)}, f32[1280,320]{0,1:T(8,128)}) fusion(f32[1280,1280]{1,0:T(8,128)} %all-gather.13.cloned.1.call-done, f32[1,1280,320]{1,2,0:T(8,128)S(1)} %copy-done), kind=kOutput, calls=%fused_computation.44 | convolution fusion | flops 3171942400 | bytes 13107200 | tf_op jit(solution)/shard_map/dot_general | solution.py:19
  175.0 20.5 %all-to-all-done.2 = f32[8,2,32,512]{3,2,1,0:T(8,128)} async-done(((f32[8,2,32,512]{3,2,1,0:T(8,128)}), f32[8,2,32,512]{3,2,1,0:T(8,128)}, u32[]{:S(2)}, u32[]{:S(2)}) %all-to-all-start.2) | async-done | bytes 1048608 | tf_op jit(solution)/shard_map/all_to_all | solution.py:35
  199.2 9.5 %all-to-all-start.3 = ((f32[2,32,512]{2,0,1:T(2,128)}), f32[2,32,512]{2,0,1:T(2,128)}, u32[]{:S(2)}, u32[]{:S(2)}) async-start(f32[2,32,512]{2,0,1:T(2,128)} %copy.47), calls=%async_computation.3 | async-start | bytes 262144 | tf_op jit(solution)/shard_map/all_to_all | solution.py:35
  211.8 4.6 all-to-all-done.3
  218.1 23.0 %all_gather.28 = f32[2,32,512]{2,0,1:T(2,128)S(1)} all-gather(f32[2,1,512]{2,0,1:T(2,128)S(1)} %maximum_add_fusion), channel_id=1, replica_groups=mesh['dp'=32,'expert'=8] {'dp'}, dimensions={1}, use_global_device_ids=true | all-gather | bytes 135168 | tf_op jit(solution)/shard_map/all_gather | solution.py:137
  250.6 18.1 %all-gather.17.cloned.1.call-done = f32[16,32,512]{2,1,0:T(8,128)} async-done(((f32[2,32,512]{2,1,0:T(8,128)}), f32[16,32,512]{2,1,0:T(8,128)}) %all-gather.17.cloned.1.call-update) | async-done | bytes 1048592 | tf_op jit(solution)/shard_map/all_gather | solution.py:39
  291.4 5.8 %fusion.11 = f32[1280,1280]{1,0:T(8,128)S(1)} fusion(f32[1280,320]{0,1:T(8,128)S(1)} %get-tuple-element.26, f32[1,1280,320]{1,2,0:T(8,128)S(1)} %copy-done), kind=kOutput, calls=%fused_computation.24 | convolution fusion | flops 3145728000 | bytes 9830400 | tf_op jit(solution)/shard_map/dot_general | solution.py:19
  297.2 5.2 %convolution_add_fusion = f32[1280,1280]{1,0:T(8,128)} fusion(f32[1280,1280]{1,0:T(8,128)S(1)} %fusion.11, f32[1280,32]{0,1:T(8,128)S(1)} %copy-done.24, f32[1280]{0:T(1024)S(1)} %get-tuple-element.25, f32[32]{0:T(128)S(1)} %copy-done.33, f32[1280,32]{0,1:T(8,128)S(1)} %get-tuple-element.43, f32[1280]{0:T(1024)S(1)} %get-tuple-element.42), kind=kOutput, calls=%fused_computation | convolution fusion | flops 316334080 | bytes 13445248 | tf_op jit(solution)/shard_map/dot_general | solution.py:19
  306.8 5.0 fusion.3
  312.6 12.7 %all-to-all-start.5 = ((f32[32,1,1280]{2,1,0:T(1,128)}), f32[32,1,1280]{2,1,0:T(1,128)S(1)}, u32[]{:S(2)}, u32[]{:S(2)}) async-start(f32[32,1,1280]{2,1,0:T(1,128)} %copy.55), calls=%async_computation.6 | async-start | bytes 327680 | tf_op jit(solution)/shard_map/all_to_all | solution.py:35
  344.5 7.4 %all-to-all-start.6 = ((f32[32,10,512]{2,1,0:T(8,128)}), f32[32,10,512]{2,1,0:T(8,128)}, u32[]{:S(2)}, u32[]{:S(2)}) async-start(f32[32,10,512]{2,1,0:T(8,128)} %reshape.278), calls=%async_computation.7 | async-start | bytes 2097152 | tf_op jit(solution)/shard_map/all_to_all | solution.py:35
  358.5 39.6 %reduce-scatter.5.cloned.1.call-done = f32[160,1280]{1,0:T(8,128)} async-done(((f32[1280,1280]{1,0:T(8,128)}), f32[160,1280]{1,0:T(8,128)}) %reduce-scatter.5.cloned.1.call-update) | async-done | bytes 819216 | tf_op jit(solution)/shard_map/reduce_scatter | solution.py:176
  400.8 7.5 %all-to-all-start.4 = ((f32[5,32,1280]{2,0,1:T(8,128)}), f32[5,32,1280]{2,0,1:T(8,128)}, u32[]{:S(2)}, u32[]{:S(2)}) async-start(f32[5,32,1280]{2,0,1:T(8,128)} %copy.53), calls=%async_computation.5 | async-start | bytes 2621440 | tf_op jit(solution)/shard_map/all_to_all | solution.py:35
  408.9 7.5 %convolution_bitcast_fusion = f32[1,1280,320]{1,2,0:T(8,128)} fusion(f32[1280,1280]{1,0:T(8,128)} %all-gather.13.cloned.1.call-done, f32[1280,320]{0,1:T(8,128)S(1)} %get-tuple-element.26), kind=kOutput, calls=%fused_computation.3 | convolution fusion | flops 3145728000 | bytes 9830400 | tf_op jit(solution)/shard_map/dot_general | solution.py:19
  416.6 19.5 %all-gather.6 = f32[8,1,1280]{2,1,0:T(1,128)S(1)} all-gather(f32[1,1,1280]{2,1,0:T(1,128)S(1)} %reshape.287), channel_id=5, replica_groups=mesh['dp'=32,'expert'=8] {'expert'}, dimensions={0}, use_global_device_ids=true | all-gather | bytes 46080 | tf_op jit(solution)/shard_map/all_gather | solution.py:39
  436.1 30.2 %all-gather.7 = f32[32,1,1280]{2,1,0:T(1,128)S(1)} all-gather(f32[1,1,1280]{2,1,0:T(1,128)S(1)} %reshape.289), channel_id=6, replica_groups=mesh['dp'=32,'expert'=8] {'dp'}, dimensions={0}, use_global_device_ids=true | all-gather | bytes 168960 | tf_op jit(solution)/shard_map/all_gather | solution.py:39
  468.3 24.3 %all-gather.8 = f32[32,10,512]{2,1,0:T(8,128)S(1)} all-gather(f32[1,10,512]{2,1,0:T(8,128)S(1)} %bitcast.178), channel_id=7, replica_groups=mesh['dp'=32,'expert'=8] {'dp'}, dimensions={0}, use_global_device_ids=true | all-gather | bytes 675840 | tf_op jit(solution)/shard_map/all_gather | solution.py:39
  (208 shorter events, 120.4 us)
Async XLA Ops:
  7.2 135.2 %copy-start = (f32[1,1280,320]{1,2,0:T(8,128)S(1)}, f32[1,1280,320]{1,2,0:T(8,128)}, u32[]{:S(2)}) copy-start(f32[1,1280,320]{1,2,0:T(8,128)} %param.9) | copy-start | bytes 4915204
  7.2 3.7 copy-start.6
  7.2 46.4 %all-gather.15.cloned.1.call-start = ((), (), s32[]{:S(2)}) async-start(), calls=%async_computation.11 | async-start | bytes 2949120 | tf_op jit(solution)/shard_map/all_gather | solution.py:39
  9.3 126.4 %all-gather.13.cloned.1.call-start = ((), (), s32[]{:S(2)}) async-start(), calls=%async_computation.9 | async-start | bytes 7372800 | tf_op jit(solution)/shard_map/all_gather | solution.py:39
  40.6 16.6 %copy-start.43 = (s32[128]{0:T(128)S(1)}, s32[128]{0:T(128)}, u32[]{:S(2)}) copy-start(s32[128]{0:T(128)} %param.13) | copy-start | bytes 1540
  40.6 17.9 %copy-start.23 = (f32[1280,32]{0,1:T(8,128)S(1)}, f32[1280,32]{0,1:T(8,128)}, u32[]{:S(2)}) copy-start(f32[1280,32]{0,1:T(8,128)} %param.8) | copy-start | bytes 491524
  40.6 19.0 %copy-start.42 = (s32[128]{0:T(128)S(1)}, s32[128]{0:T(128)}, u32[]{:S(2)}) copy-start(s32[128]{0:T(128)} %param.12) | copy-start | bytes 1540
  53.6 43.6 %collective-permute-start = (f32[1280,512]{1,0:T(8,128)}, f32[1280,512]{1,0:T(8,128)}, u32[]{:S(2)}, u32[]{:S(2)}) collective-permute-start(f32[1280,512]{1,0:T(8,128)} %bitcast.169), channel_id=1, source_target_pairs={{0,8},{8,0},{16,24},{24,16},{32,40},{40,32},{48,56},{56,48},{64,72... | collective-permute-start | bytes 7864328 | tf_op jit(solution)/shard_map/ppermute | solution.py:59
  57.9 112.0 %copy-start.36 = (f32[1,128]{1,0:T(1,128)}, f32[1,128]{1,0:T(1,128)S(1)}, u32[]{:S(2)}) copy-start(f32[1,128]{1,0:T(1,128)S(1)} %get-tuple-element.38) | copy-start | bytes 1540
  59.3 37.8 %copy-start.30 = (f32[128]{0:T(128)}, f32[128]{0:T(128)S(1)}, u32[]{:S(2)}) copy-start(f32[128]{0:T(128)S(1)} %get-tuple-element.39) | copy-start | bytes 1540
  60.4 13.9 %all-to-all-start.1 = ((f32[32,1,128]{2,1,0:T(1,128)}), f32[32,1,128]{2,1,0:T(1,128)S(1)}, u32[]{:S(2)}, u32[]{:S(2)}) async-start(f32[32,1,128]{2,1,0:T(1,128)} %bitcast.9), calls=%async_computation.1 | async-start | bytes 32768 | tf_op jit(solution)/shard_map/all_to_all | solution.py:35
  67.4 74.2 %copy-start.32 = (f32[32]{0:T(128)}, f32[32]{0:T(128)S(1)}, u32[]{:S(2)}) copy-start(f32[32]{0:T(128)S(1)} %compare_convert_fusion.1) | copy-start | bytes 388
  164.2 31.3 %all-to-all-start.2 = ((f32[8,2,32,512]{3,2,1,0:T(8,128)}), f32[8,2,32,512]{3,2,1,0:T(8,128)}, u32[]{:S(2)}, u32[]{:S(2)}) async-start(f32[8,2,32,512]{3,2,1,0:T(8,128)} %copy.46), calls=%async_computation.2 | async-start | bytes 2097152 | tf_op jit(solution)/shard_map/all_to_all | solution.py:35
  199.2 17.3 %all-to-all-start.3 = ((f32[2,32,512]{2,0,1:T(2,128)}), f32[2,32,512]{2,0,1:T(2,128)}, u32[]{:S(2)}, u32[]{:S(2)}) async-start(f32[2,32,512]{2,0,1:T(2,128)} %copy.47), calls=%async_computation.3 | async-start | bytes 262144 | tf_op jit(solution)/shard_map/all_to_all | solution.py:35
  208.7 60.0 %all-gather.17.cloned.1.call-start = ((), (), s32[]{:S(2)}) async-start(), calls=%async_computation.12 | async-start | bytes 1179648 | tf_op jit(solution)/shard_map/all_gather | solution.py:39
  241.7 96.8 %reduce-scatter.7.cloned.1.call-start = ((), (), s32[]{:S(2)}) async-start(), calls=%async_computation.13 | async-start | bytes 2949120
  250.4 147.7 %reduce-scatter.5.cloned.1.call-start = ((), (), s32[]{:S(2)}) async-start(), calls=%async_computation.10 | async-start | bytes 7372800 | tf_op jit(solution)/shard_map/reduce_scatter | solution.py:176
  291.3 5.9 %copy-start.24 = (f32[1280,32]{0,1:T(8,128)S(1)}, f32[1280,32]{0,1:T(8,128)}, u32[]{:S(2)}) copy-start(f32[1280,32]{0,1:T(8,128)} %param.8) | copy-start | bytes 491524
  291.3 5.9 %copy-start.33 = (f32[32]{0:T(128)S(1)}, f32[32]{0:T(128)}, u32[]{:S(2)}) copy-start(f32[32]{0:T(128)} %copy-done.32) | copy-start | bytes 388
  312.6 32.0 %all-to-all-start.5 = ((f32[32,1,1280]{2,1,0:T(1,128)}), f32[32,1,1280]{2,1,0:T(1,128)S(1)}, u32[]{:S(2)}, u32[]{:S(2)}) async-start(f32[32,1,1280]{2,1,0:T(1,128)} %copy.55), calls=%async_computation.6 | async-start | bytes 327680 | tf_op jit(solution)/shard_map/all_to_all | solution.py:35
  344.5 56.3 %all-to-all-start.6 = ((f32[32,10,512]{2,1,0:T(8,128)}), f32[32,10,512]{2,1,0:T(8,128)}, u32[]{:S(2)}, u32[]{:S(2)}) async-start(f32[32,10,512]{2,1,0:T(8,128)} %reshape.278), calls=%async_computation.7 | async-start | bytes 2097152 | tf_op jit(solution)/shard_map/all_to_all | solution.py:35
  352.0 3.7 copy-start.2
  352.0 3.7 copy-start.22
  400.8 92.7 %all-to-all-start.4 = ((f32[5,32,1280]{2,0,1:T(8,128)}), f32[5,32,1280]{2,0,1:T(8,128)}, u32[]{:S(2)}, u32[]{:S(2)}) async-start(f32[5,32,1280]{2,0,1:T(8,128)} %copy.53), calls=%async_computation.5 | async-start | bytes 2621440 | tf_op jit(solution)/shard_map/all_to_all | solution.py:35
  (32 other events, 67.8 us)
Sparse Core Ops, SparseCore 0:
  10.4 43.1 all-gather.14
  55.9 79.7 all-gather.12
  241.9 26.7 all-gather.16
  271.1 43.6 reduce-scatter.6
  317.1 80.8 reduce-scatter.4
